TPU v7x, 32 devices: a whole 2x2x4 slice. The times are simulated.
32 devices in a mesh: dp: 16 (over z, y, x), tensor: 2 (over core).
Axes of the slice: x: 2, y: 2, z: 4, core: 2. Of those that a mesh axis runs over, the one named last changes fastest.
Arguments:
- block_input: bfloat16 [4096, 1024], P('dp'), may hold values from -6 to 6
- cotangent: bfloat16 [4096, 1024], P('dp'), may hold values from -6 to 6
- seq_lengths: int32 [16, 4], P('dp'), may hold values from 0 to 256, as said below
- ln1_gain: float32 [1024], replicated, may hold values from 0.1 to 1.9
- ln1_bias: float32 [1024], replicated, may hold values from -4 to 4
- w_qkv: bfloat16 [3, 1024, 1024], P(None, None, 'tensor'), may hold values from -0.1875 to 0.1875
- qv_bias: float32 [2, 1024], P(None, 'tensor'), may hold values from -6 to 6
- w_out: bfloat16 [1024, 1024], P('tensor'), may hold values from -0.75 to 0.75
- out_bias: float32 [1024], replicated, may hold values from -6 to 6
- ln2_gain: float32 [1024], replicated, may hold values from 0.1 to 1.9
- ln2_bias: float32 [1024], replicated, may hold values from -4 to 4
- w_fc: bfloat16 [1024, 4096], P(None, 'tensor'), may hold values from -0.1875 to 0.1875
- fc_bias: float32 [4096], P('tensor'), may hold values from -6 to 6
- w_proj: bfloat16 [4096, 1024], P('tensor'), may hold values from -0.09375 to 0.09375
- proj_bias: float32 [1024], replicated, may hold values from -6 to 6
Outputs:
- block_output: bfloat16 [4096, 1024], P('dp')
- input_grad: bfloat16 [4096, 1024], P('dp')
- ln1_gain_grad: float32 [1024], replicated
- ln1_bias_grad: float32 [1024], replicated
- w_qkv_grad: float32 [3, 1024, 1024], P(None, None, 'tensor')
- qv_bias_grad: float32 [2, 1024], P(None, 'tensor')
- w_out_grad: float32 [1024, 1024], P('tensor')
- out_bias_grad: float32 [1024], replicated
- ln2_gain_grad: float32 [1024], replicated
- ln2_bias_grad: float32 [1024], replicated
- w_fc_grad: float32 [1024, 4096], P(None, 'tensor')
- fc_bias_grad: float32 [4096], P('tensor')
- w_proj_grad: float32 [4096, 1024], P('tensor')
- proj_bias_grad: float32 [1024], replicated
Inputs may be any that keep to these rules, and one draw needn't show every extreme that they name: `seq_lengths`: row i lists the lengths of the 4 sequences packed in order from the first row of data index i; a row sums to at most 256, the rows after them are padding, lengths may be zero, and in every draw some row holds one sequence of 256 tokens.
All inputs are finite; a program needn't handle non-finite values.
Results may differ from a plain program's by a relative error of at most 0.012.
Values sent between devices are 32-bit elements; how exact they have to be, the bound alone decides.
A program may use at most 192 MiB of HBM per device.

v0:
```python
import jax
import jax.numpy as jnp
from jax import lax
from jax.sharding import PartitionSpec as P

HEAD_DIM = 64


EPS = 1e-05
GELU_SCALE = 0.7978845608028654
SCORE_SCALE = 0.125


def layer_norm(values, gain, shift):
    centre = jnp.mean(values, axis=-1, keepdims=True)
    centred = values - centre
    spread = jnp.mean(centred * centred, axis=-1, keepdims=True)
    return centred * lax.rsqrt(spread + EPS) * gain + shift


def gelu(values):
    return (
        0.5 * values * (1.0 + jnp.tanh(GELU_SCALE * (values + 0.044715 * values * values * values)))
    )


def flatten_all(arrays, groups):
    flat = jnp.concatenate([item.reshape(-1) for item in arrays])
    length = flat.shape[0]
    padded = -(-length // groups) * groups
    return (flat, padded)


def restore_all(flat, arrays):
    result = []
    offset = 0
    for item in arrays:
        result.append(flat[offset : offset + item.size].reshape(item.shape))
        offset = offset + item.size
    return result


def per_device(
    block_input,
    cotangent,
    seq_lengths,
    ln1_gain,
    ln1_bias,
    w_qkv,
    qv_bias,
    w_out,
    out_bias,
    ln2_gain,
    ln2_bias,
    w_fc,
    fc_bias,
    w_proj,
    proj_bias,
):
    rows = block_input.shape[0]
    local_width = w_qkv.shape[2]
    heads = local_width // HEAD_DIM
    groups = lax.axis_size("dp")
    ends = jnp.cumsum(seq_lengths[0])
    position = jnp.arange(rows, dtype=jnp.int32)
    segment = jnp.sum((position[:, None] >= ends[None, :]).astype(jnp.int32), axis=1)
    valid = (segment < seq_lengths.shape[1]).astype(jnp.float32)
    inputs = block_input.astype(jnp.float32)
    normed_one = layer_norm(inputs, ln1_gain, ln1_bias).astype(jnp.bfloat16)
    projected = jnp.einsum("td,cdh->cth", normed_one, w_qkv, preferred_element_type=jnp.float32)
    queries = (projected[0] + qv_bias[0]).astype(jnp.bfloat16)
    keys = projected[1].astype(jnp.bfloat16)
    values = (projected[2] + qv_bias[1]).astype(jnp.bfloat16)
    query_heads = queries.reshape(rows, heads, HEAD_DIM)
    key_heads = keys.reshape(rows, heads, HEAD_DIM)
    value_heads = values.reshape(rows, heads, HEAD_DIM)

    def scores_of():
        scores = (
            jnp.einsum("qhe,khe->hqk", query_heads, key_heads, preferred_element_type=jnp.float32)
            * SCORE_SCALE
        )
        allowed = (segment[:, None] == segment[None, :]) & (position[None, :] <= position[:, None])
        return jnp.where(allowed[None], scores, jnp.float32(-1e30))

    scores = scores_of()
    row_max = jnp.max(scores, axis=-1, keepdims=True)
    expd = jnp.exp(scores - row_max)
    total = jnp.sum(expd, axis=-1, keepdims=True)
    probs = expd / total
    log_totals = row_max + jnp.log(total)
    pieces = jnp.einsum(
        "hqk,khe->qhe", probs.astype(jnp.bfloat16), value_heads, preferred_element_type=jnp.float32
    )
    attended = pieces.reshape(rows, local_width).astype(jnp.bfloat16)
    branch = (
        lax.psum(jnp.dot(attended, w_out, preferred_element_type=jnp.float32), "tensor") + out_bias
    )
    residual = inputs + branch
    normed_two = layer_norm(residual, ln2_gain, ln2_bias).astype(jnp.bfloat16)
    hidden_pre = jnp.dot(normed_two, w_fc, preferred_element_type=jnp.float32) + fc_bias
    hidden = gelu(hidden_pre).astype(jnp.bfloat16)
    mlp_out = (
        lax.psum(jnp.dot(hidden, w_proj, preferred_element_type=jnp.float32), "tensor") + proj_bias
    )
    block_output = (residual + mlp_out).astype(jnp.bfloat16)
    grad_out = cotangent.astype(jnp.float32) * valid[:, None]
    grad_mlp = grad_out.astype(jnp.bfloat16)
    proj_bias_grad = jnp.sum(grad_mlp.astype(jnp.float32), axis=0)
    w_proj_grad = jnp.einsum("tf,td->fd", hidden, grad_mlp, preferred_element_type=jnp.float32)
    grad_act = jnp.einsum("td,fd->tf", grad_mlp, w_proj, preferred_element_type=jnp.float32)
    grad_hidden = jax.vjp(gelu, hidden_pre)[1](grad_act)[0].astype(jnp.bfloat16)
    fc_bias_grad = jnp.sum(grad_hidden.astype(jnp.float32), axis=0)
    w_fc_grad = jnp.einsum("td,tf->df", normed_two, grad_hidden, preferred_element_type=jnp.float32)
    mlp_list = [w_fc_grad, fc_bias_grad, w_proj_grad, proj_bias_grad]
    grad_normed_two = lax.psum(
        jnp.einsum("tf,df->td", grad_hidden, w_fc, preferred_element_type=jnp.float32), "tensor"
    )
    grad_res_ln, ln2_gain_grad, ln2_bias_grad = jax.vjp(layer_norm, residual, ln2_gain, ln2_bias)[
        1
    ](grad_normed_two)
    grad_residual = grad_out + grad_res_ln
    grad_branch = grad_residual.astype(jnp.bfloat16)
    out_bias_grad = jnp.sum(grad_branch.astype(jnp.float32), axis=0)
    w_out_grad = jnp.einsum("th,td->hd", attended, grad_branch, preferred_element_type=jnp.float32)
    grad_attended = jnp.einsum("td,hd->th", grad_branch, w_out, preferred_element_type=jnp.float32)
    grad_attended = grad_attended.astype(jnp.bfloat16).reshape(rows, heads, HEAD_DIM)
    probs = jnp.exp(scores_of() - log_totals)
    grad_probs = jnp.einsum(
        "qhe,khe->hqk", grad_attended, value_heads, preferred_element_type=jnp.float32
    )
    inner = jnp.sum(probs * grad_probs, axis=-1, keepdims=True)
    grad_scores = (probs * (grad_probs - inner)).astype(jnp.bfloat16)
    query_pieces = (
        jnp.einsum("hqk,khe->qhe", grad_scores, key_heads, preferred_element_type=jnp.float32)
        * SCORE_SCALE
    )
    grad_keys = (
        jnp.einsum("hqk,qhe->khe", grad_scores, query_heads, preferred_element_type=jnp.float32)
        * SCORE_SCALE
    )
    grad_values = jnp.einsum(
        "hqk,qhe->khe",
        probs.astype(jnp.bfloat16),
        grad_attended,
        preferred_element_type=jnp.float32,
    )
    grad_queries = query_pieces.reshape(rows, local_width).astype(jnp.bfloat16)
    grad_keys = grad_keys.reshape(rows, local_width).astype(jnp.bfloat16)
    grad_values = grad_values.reshape(rows, local_width).astype(jnp.bfloat16)
    grad_stack = jnp.stack([grad_queries, grad_keys, grad_values], axis=0)
    qv_bias_grad = jnp.stack(
        [
            jnp.sum(grad_queries.astype(jnp.float32), axis=0),
            jnp.sum(grad_values.astype(jnp.float32), axis=0),
        ],
        axis=0,
    )
    w_qkv_grad = jnp.einsum(
        "td,cth->cdh", normed_one, grad_stack, preferred_element_type=jnp.float32
    )
    grad_normed_one = lax.psum(
        jnp.einsum("cth,cdh->td", grad_stack, w_qkv, preferred_element_type=jnp.float32), "tensor"
    )
    grad_in_ln, ln1_gain_grad, ln1_bias_grad = jax.vjp(layer_norm, inputs, ln1_gain, ln1_bias)[1](
        grad_normed_one
    )
    input_grad = (grad_residual + grad_in_ln).astype(jnp.bfloat16)
    attn_list = [
        ln1_gain_grad,
        ln1_bias_grad,
        w_qkv_grad,
        qv_bias_grad,
        w_out_grad,
        out_bias_grad,
        ln2_gain_grad,
        ln2_bias_grad,
    ]
    total_flat, total_padded = flatten_all(attn_list + mlp_list, groups)
    share = lax.psum_scatter(total_flat, "dp", scatter_dimension=0, tiled=True)
    gathered = lax.all_gather(share, "dp", axis=0, tiled=True)
    summed = restore_all(gathered, attn_list + mlp_list)
    return (
        block_output,
        input_grad,
        summed[0],
        summed[1],
        summed[2],
        summed[3],
        summed[4],
        summed[5],
        summed[6],
        summed[7],
        summed[8],
        summed[9],
        summed[10],
        summed[11],
    )


def solution(mesh):
    return jax.shard_map(
        per_device,
        mesh=mesh,
        in_specs=(
            P("dp", None),
            P("dp", None),
            P("dp", None),
            P(),
            P(),
            P(None, None, "tensor"),
            P(None, "tensor"),
            P("tensor", None),
            P(),
            P(),
            P(),
            P(None, "tensor"),
            P("tensor"),
            P("tensor", None),
            P(),
        ),
        out_specs=(
            P("dp", None),
            P("dp", None),
            P(),
            P(),
            P(None, None, "tensor"),
            P(None, "tensor"),
            P("tensor", None),
            P(),
            P(),
            P(),
            P(None, "tensor"),
            P("tensor"),
            P("tensor", None),
            P(),
        ),
        check_vma=False,
    )
```

profile of v0, /device:TPU:0, one launch (start us, length us, event | category | flops | bytes accessed | tf_op | source)
XLA Modules:
  0.0 1568.0 jit_solution(6729880049467788454)
XLA Ops:
  9.9 2.1 convolution_bitcast_fusion.4
  13.9 2.1 copy.70
  24.9 22.4 %all-reduce.9.cloned.1.call-done = f32[256,1024]{1,0:T(8,128)} async-done(((f32[256,1024]{1,0:T(8,128)}), f32[256,1024]{1,0:T(8,128)}) %all-reduce.9.cloned.1.call-update) | async-done | bytes 1048592 | tf_op jit(solution)/shard_map/psum | solution.py:97
  49.9 3.7 convolution_add_fusion
  53.6 4.4 convert_reduce_fusion
  59.0 2.3 fusion.51
  61.6 5.3 fusion.40
  66.9 15.4 all-reduce.11.cloned.1.call-done
  82.3 2.0 multiply_reduce_fusion.1
  89.3 2.6 multiply_reduce_fusion
  100.9 3.0 convolution_bitcast_fusion.5
  106.9 5.5 copy.90
  114.1 5.5 copy.91
  119.7 4.0 convolution_bitcast_fusion.2
  123.7 6.7 copy.81
  130.4 7.2 copy.87
  143.4 5.4 constant_dynamic-update-slice_fusion.9
  152.7 4.4 constant_dynamic-update-slice_fusion.3
  159.0 3.7 constant_dynamic-update-slice_fusion.1
  165.8 658.8 %all-reduce.15.cloned.1.call-done = f32[6300672]{0:T(1024)} async-done(((f32[6300672]{0:T(1024)}), f32[6300672]{0:T(1024)}) %all-reduce.15.cloned.1.call-update) | async-done | bytes 25202704
  824.6 3.0 dynamic-slice.2
  827.6 8.6 broadcast.145
  836.2 14.7 dynamic-update-slice
  851.6 2.2 add_convert_fusion.1
  855.1 655.0 %all-reduce.13.cloned.1.call-done = f32[6300672]{0:T(1024)} async-done(((f32[6300672]{0:T(1024)}), f32[6300672]{0:T(1024)}) %all-reduce.13.cloned.1.call-update) | async-done | bytes 25202704
  1510.1 11.8 fusion.46
  1522.0 9.2 reshape.293
  1531.2 9.2 slice.100
  1540.4 4.7 slice.107
  1545.2 7.1 reshape.292
  1552.3 3.2 slice.109
  1555.5 2.7 slice.93
  (174 shorter events, 54.2 us)
Async XLA Ops:
  7.2 40.1 %all-reduce.9.cloned.1.call-start = ((), (), s32[]{:S(2)}) async-start(), calls=%async_computation | async-start | bytes 2097152 | tf_op jit(solution)/shard_map/psum | solution.py:97
  12.1 4.9 copy-start.39
  12.1 5.1 copy-start.44
  17.0 4.6 copy-start.24
  22.7 24.6 %copy-start.36 = (f32[1024]{0:T(1024)S(1)}, f32[1024]{0:T(1024)}, u32[]{:S(2)}) copy-start(f32[1024]{0:T(1024)} %param.23) | copy-start | bytes 12292
  24.8 25.0 %copy-start.33 = (f32[1024]{0:T(1024)S(1)}, f32[1024]{0:T(1024)}, u32[]{:S(2)}) copy-start(f32[1024]{0:T(1024)} %param.24) | copy-start | bytes 12292
  24.9 25.0 %copy-start.34 = (f32[1024]{0:T(1024)S(1)}, f32[1024]{0:T(1024)}, u32[]{:S(2)}) copy-start(f32[1024]{0:T(1024)} %param.25) | copy-start | bytes 12292
  24.9 25.0 %copy-start.43 = (f32[2048]{0:T(1024)S(1)}, f32[2048]{0:T(1024)}, u32[]{:S(2)}) copy-start(f32[2048]{0:T(1024)} %param.27) | copy-start | bytes 24580
  24.9 57.4 %all-reduce.11.cloned.1.call-start = ((), (), s32[]{:S(2)}) async-start(), calls=%async_computation.1 | async-start | bytes 2097152 | tf_op jit(solution)/shard_map/psum | solution.py:116
  49.9 3.7 copy-start.13
  49.9 3.7 copy-start.42
  53.6 4.5 copy-start.22
  53.6 5.4 copy-start.41
  61.3 78.7 %all-reduce.17.cloned.1.call-start = ((), (), s32[]{:S(2)}) async-start(), calls=%async_computation.4 | async-start | bytes 4194304 | tf_op jit(solution)/shard_map/psum | solution.py:104
  104.0 720.6 %all-reduce.15.cloned.1.call-start = ((), (), s32[]{:S(2)}) async-start(), calls=%async_computation.3 | async-start | bytes 50405376
  106.9 5.5 copy-start.15
  106.9 5.5 copy-start.23
  114.1 5.6 copy-start.7
  114.1 5.6 copy-start.29
  114.1 5.5 copy-start.30
  114.1 5.5 copy-start.35
  114.1 5.5 copy-start.37
  130.4 7.4 copy-start.17
  130.4 7.4 copy-start.32
  143.4 9.3 slice-start.2
  143.4 6.0 copy-start.12
  143.4 9.3 slice-start.3
  152.7 5.0 slice-start
  152.7 6.4 slice-start.1
  163.3 1346.8 %all-reduce.13.cloned.1.call-start = ((), (), s32[]{:S(2)}) async-start(), calls=%async_computation.2 | async-start | bytes 50405376
  850.9 2.9 copy-start.9
  1552.3 9.2 copy-start.1
  (22 other events, 34.7 us)
Sparse Core Ops, SparseCore 0:
  25.0 22.2 all-reduce.8
  61.4 20.7 all-reduce.10
  104.1 22.4 all-reduce.16
  163.4 661.0 all-reduce.14
  851.0 659.0 all-reduce.12
where the time goes:
time: 1570 us
  waiting for transfers between devices  1350 us (86%)
  local copies, waits for them, and re-layouts  147 us (9%)
  matrix products  39.2 us (2%)
    unnamed x7, waiting for transfers between devices  1310 us
    unnamed x118, local copies, waits for them, and re-layouts  75.2 us
    slice x8, local copies, waits for them, and re-layouts, restore_all(): result.append(flat[offset:offset + item.size].reshape(item.shape))  34.9 us
  transfers between devices with their start and end apart: 5, of which 4 were waited for; matrix products, arithmetic and copies ran while one was open for 3% of the time, Pallas kernels for 0%

commit v1 on v0

--- a/solution.py
+++ b/solution.py
@@ -1,6 +1,10 @@
+import functools
+
 import jax
 import jax.numpy as jnp
 from jax import lax
+from jax.experimental import pallas as pl
+from jax.experimental.pallas import tpu as pltpu
 from jax.sharding import PartitionSpec as P
 
 HEAD_DIM = 64
@@ -24,20 +28,362 @@
     )
 
 
-def flatten_all(arrays, groups):
-    flat = jnp.concatenate([item.reshape(-1) for item in arrays])
-    length = flat.shape[0]
-    padded = -(-length // groups) * groups
-    return (flat, padded)
-
-
-def restore_all(flat, arrays):
-    result = []
-    offset = 0
-    for item in arrays:
-        result.append(flat[offset : offset + item.size].reshape(item.shape))
-        offset = offset + item.size
-    return result
+MESH = pl.DeviceIdType.MESH
+CUTS = 4
+ORDERS = ("xyz", "yzx", "zxy", "zxy", "xyz")
+PIECES = (CUTS, CUTS, CUTS, CUTS, 1)
+
+
+class Stream:
+    def __init__(self, shape, order, pieces):
+        self.order, self.pieces = order, pieces
+        self.cell_rows = shape[0] // 8
+        self.rows = self.cell_rows // pieces
+        self.columns = shape[1]
+        self.slots = [
+            (2 if axis == "z" else 1) * 2 ** (2 - step) for step, axis in enumerate(order)
+        ]
+        self.held = 8 if order[0] == "z" else 4
+        self.offsets = []
+        total = 0
+        for _ in range(2):
+            for count in self.slots:
+                self.offsets.append(total)
+                total += count * pieces
+        self.semaphores = total
+
+    def scratch(self):
+        shape = (self.cell_rows, self.columns)
+        return (
+            [pltpu.VMEM((self.held,) + shape, jnp.float32)]
+            + [pltpu.VMEM((count,) + shape, jnp.float32) for count in self.slots]
+            + [
+                pltpu.SemaphoreType.DMA((self.semaphores,)),
+                pltpu.SemaphoreType.DMA((self.semaphores,)),
+                pltpu.SemaphoreType.DMA((self.held,)),
+                pltpu.SemaphoreType.DMA((self.pieces,)),
+            ]
+        )
+
+    def bind(self, source, result, held, one, two, three, send, recv, load, store):
+        self.source, self.result, self.acc = source, result, held
+        self.landing = (one, two, three)
+        self.send, self.recv, self.load, self.store = send, recv, load, store
+
+
+def reduce_kernel(streams, *refs):
+    count = len(streams)
+    for number, stream in enumerate(streams):
+        first = 2 * count + 8 * number
+        stream.bind(refs[number], refs[count + number], *refs[first : first + 8])
+    me = lax.axis_index("dp")
+    other_axis = lax.axis_index("tensor")
+    x, y, z = lax.rem(me, 2), lax.rem(me // 2, 2), me // 4
+    mine = {"x": x, "y": y, "z": z // 2}
+    other = {"x": 1 - x, "y": 1 - y}
+    below, above = me - 4, me + 4
+    partner = {"x": me + 1 - 2 * x, "y": me + 2 - 4 * y}
+    at_end = (z == 0) | (z == 3)
+    inside = (z == 1) | (z == 2)
+    at = {0: z == 0, 1: z == 3}
+    away = {0: z != 0, 1: z != 3}
+    drains = []
+
+    def device(index):
+        return (index, other_axis)
+
+    def span(stream, k):
+        start = k * stream.rows
+        return pl.ds(pl.multiple_of(start, 8), stream.rows)
+
+    def in_hbm(stream, ref, bits, k):
+        cell = 4 * bits["x"] + 2 * bits["y"] + bits["z"]
+        start = cell * stream.cell_rows + k * stream.rows
+        return ref.at[pl.ds(pl.multiple_of(start, 8), stream.rows)]
+
+    def held_slot(stream, bits):
+        a, b, c = stream.order
+        low = 2 * bits[b] + bits[c]
+        return 4 * bits[a] + low if stream.held == 8 else low
+
+    def in_acc(stream, bits, k):
+        return stream.acc.at[held_slot(stream, bits), span(stream, k)]
+
+    def step_slot(stream, step, bits):
+        slot = 0
+        for axis in stream.order[step + 1 :]:
+            slot = 2 * slot + bits[axis]
+        if stream.order[step] == "z":
+            slot = slot + bits["z"] * 2 ** (2 - step)
+        return slot
+
+    def landing(stream, step, bits, k):
+        return stream.landing[step].at[step_slot(stream, step, bits), span(stream, k)]
+
+    def remote(stream, phase, step, bits, k, src, dst, to):
+        index = stream.offsets[3 * phase + step] + step_slot(stream, step, bits) * stream.pieces + k
+        return pltpu.make_async_remote_copy(
+            src_ref=src,
+            dst_ref=dst,
+            send_sem=stream.send.at[index],
+            recv_sem=stream.recv.at[index],
+            device_id=device(to),
+            device_id_type=MESH,
+        )
+
+    def guarded(condition, work):
+        if condition is None:
+            work()
+        else:
+            pl.when(condition)(work)
+
+    def scatter_copy(stream, step, bits, from_input):
+        axis = stream.order[step]
+        to = partner[axis] if axis != "z" else (below if bits["z"] == 0 else above)
+
+        def make(k):
+            src = in_hbm(stream, stream.source, bits, k) if from_input else in_acc(stream, bits, k)
+            return remote(stream, 0, step, bits, k, src, landing(stream, step, bits, k), to)
+
+        return make
+
+    def gather_copy(stream, step, bits, from_acc):
+        axis = stream.order[step]
+        to = partner[axis] if axis != "z" else (above if bits["z"] == 0 else below)
+
+        def make(k):
+            dst = in_hbm(stream, stream.result, bits, k)
+            src = in_acc(stream, bits, k) if from_acc else in_hbm(stream, stream.result, bits, k)
+            return remote(stream, 1, step, bits, k, src, dst, to)
+
+        return make
+
+    def later_bits(stream, step):
+        settings = [({}, {})]
+        for axis in stream.order[step + 1 :]:
+            grown = []
+            for bits, tags in settings:
+                for tag in (1, 0):
+                    if axis == "z":
+                        value = 1 - tag
+                    else:
+                        value = other[axis] if tag else mine[axis]
+                    grown.append(({**bits, axis: value}, {**tags, axis: tag}))
+            settings = grown
+        return settings
+
+    def full(stream, step, later):
+        bits = {axis: mine[axis] for axis in stream.order[:step]}
+        return {**bits, **later}
+
+    def only_ends(stream, step):
+        return at_end if "z" in stream.order[:step] else None
+
+    def send(stream, k, make, condition):
+        guarded(condition, lambda: make(k).start())
+        drains.append((stream.pieces, make, condition))
+
+    def ready(stream, step, bits, tags, k, condition):
+        if step == 3:
+            own = pltpu.make_async_copy(
+                in_acc(stream, bits, k),
+                in_hbm(stream, stream.result, bits, k),
+                stream.store.at[k],
+            )
+            guarded(condition, own.start)
+            for ahead in (2, 1, 0):
+                if stream.order[ahead] != "z":
+                    send(stream, k, gather_copy(stream, ahead, bits, True), condition)
+                else:
+                    for end in (0, 1):
+                        cell = {**bits, "z": end}
+                        send(stream, k, gather_copy(stream, ahead, cell, True), at[end])
+            return
+        axis = stream.order[step]
+        if axis == "z":
+            end = bits["z"]
+            send(stream, k, scatter_copy(stream, step, bits, False), at[1 - end])
+        elif tags[axis]:
+            send(stream, k, scatter_copy(stream, step, bits, False), condition)
+
+    def add_landed(stream, step, bits, k):
+        remote(
+            stream, 0, step, bits, k, in_acc(stream, bits, k), landing(stream, step, bits, k), me
+        ).wait_recv()
+        slot, place = held_slot(stream, bits), step_slot(stream, step, bits)
+
+        @pl.loop(0, stream.rows // 8)
+        def _(row):
+            rows = pl.ds(pl.multiple_of(k * stream.rows + row * 8, 8), 8)
+            stream.acc[slot, rows] = stream.acc[slot, rows] + stream.landing[step][place, rows]
+
+    def scatter(stream, step, later, tags, k):
+        axis = stream.order[step]
+        ends = only_ends(stream, step)
+        if axis != "z":
+            bits = full(stream, step, {**later, axis: mine[axis]})
+            guarded(ends, lambda: add_landed(stream, step, bits, k))
+            ready(stream, step + 1, bits, tags, k, ends)
+            return
+        for end in (0, 1):
+            bits = full(stream, step, {**later, "z": end})
+            guarded(away[1 - end], lambda bits=bits: add_landed(stream, step, bits, k))
+            send(stream, k, scatter_copy(stream, step, bits, False), inside)
+        if step == 2:
+            bits = full(stream, step, {**later, "z": mine["z"]})
+            ready(stream, 3, bits, tags, k, at_end)
+        else:
+            for end in (0, 1):
+                axis = stream.order[step + 1]
+                if tags[axis]:
+                    bits = full(stream, step, {**later, "z": end})
+                    send(stream, k, scatter_copy(stream, step + 1, bits, False), at[end])
+
+    def gather(stream, step, later, k):
+        axis = stream.order[step]
+        ends = only_ends(stream, step)
+
+        def landed(bits):
+            here = in_hbm(stream, stream.result, bits, k)
+            remote(stream, 1, step, bits, k, here, here, me).wait_recv()
+
+        def onward(bits, condition):
+            for ahead in range(step - 1, -1, -1):
+                if stream.order[ahead] != "z":
+                    send(stream, k, gather_copy(stream, ahead, bits, False), condition)
+                else:
+                    for end in (0, 1):
+                        cell = {**bits, "z": end}
+                        send(stream, k, gather_copy(stream, ahead, cell, False), at[end])
+
+        if axis != "z":
+            bits = full(stream, step, {**later, axis: other[axis]})
+            guarded(ends, lambda: landed(bits))
+            onward(bits, ends)
+            return
+        for end in (0, 1):
+            bits = full(stream, step, {**later, "z": end})
+            guarded(away[end], lambda bits=bits: landed(bits))
+            send(stream, k, gather_copy(stream, step, bits, False), inside)
+            onward(bits, away[end])
+
+    def loads(stream):
+        a, b, c = stream.order
+        for slot in range(stream.held):
+            bits = {b: (slot // 2) % 2, c: slot % 2, a: slot // 4 if stream.held == 8 else mine[a]}
+            cell = 4 * bits["x"] + 2 * bits["y"] + bits["z"]
+            start = pl.multiple_of(cell * stream.cell_rows, 8)
+            yield pltpu.make_async_copy(
+                stream.source.at[pl.ds(start, stream.cell_rows)],
+                stream.acc.at[slot],
+                stream.load.at[slot],
+            )
+
+    barrier = pltpu.get_barrier_semaphore()
+
+    def greet(index):
+        pl.semaphore_signal(barrier, inc=1, device_id=device(index), device_id_type=MESH)
+
+    for stream in streams:
+        for copy in loads(stream):
+            copy.start()
+    greet(partner["x"])
+    greet(partner["y"])
+    pl.when(z > 0)(lambda: greet(below))
+    pl.when(z < 3)(lambda: greet(above))
+    pl.semaphore_wait(barrier, 3 + inside.astype(jnp.int32))
+
+    big = [stream for stream in streams if stream.pieces > 1]
+    little = [stream for stream in streams if stream.pieces == 1]
+
+    def each(step, work):
+        settings = {id(stream): later_bits(stream, step) for stream in streams}
+        for turn in range(2 ** (2 - step)):
+            for stream in little:
+                work(stream, step, *settings[id(stream)][turn], 0)
+
+            @pl.loop(0, CUTS)
+            def _(k):
+                for stream in big:
+                    work(stream, step, *settings[id(stream)][turn], k)
+
+    def first(stream, step, later, tags, k):
+        axis = stream.order[0]
+        if axis == "z":
+            for end in (0, 1):
+                bits = {**later, "z": end}
+                send(stream, k, scatter_copy(stream, 0, bits, True), at[1 - end])
+        else:
+            bits = {**later, axis: other[axis]}
+            send(stream, k, scatter_copy(stream, 0, bits, True), None)
+
+    each(0, first)
+    for stream in streams:
+        for copy in loads(stream):
+            copy.wait()
+    for step in (0, 1, 2):
+        each(step, scatter)
+    for step in (2, 1, 0):
+        each(step, lambda stream, step, later, tags, k: gather(stream, step, later, k))
+
+    for pieces, make, condition in drains:
+
+        def drain(pieces=pieces, make=make):
+            @pl.loop(0, pieces)
+            def _(k):
+                make(k).wait_send()
+
+        guarded(condition, drain)
+    for stream in streams:
+        bits = dict(mine)
+
+        def stored(stream=stream, bits=bits):
+            @pl.loop(0, stream.pieces)
+            def _(k):
+                pltpu.make_async_copy(
+                    in_acc(stream, bits, k),
+                    in_hbm(stream, stream.result, bits, k),
+                    stream.store.at[k],
+                ).wait()
+
+        pl.when(at_end)(stored)
+
+
+def sum_over_data(arrays):
+    streams = [
+        Stream(item.shape, order, pieces)
+        for item, order, pieces in zip(arrays, ORDERS, PIECES, strict=True)
+    ]
+    size = sum(item.size for item in arrays)
+    return pl.pallas_call(
+        functools.partial(reduce_kernel, streams),
+        out_shape=[jax.ShapeDtypeStruct(item.shape, item.dtype) for item in arrays],
+        in_specs=[pl.BlockSpec(memory_space=pl.ANY)] * len(arrays),
+        out_specs=[pl.BlockSpec(memory_space=pl.ANY)] * len(arrays),
+        scratch_shapes=[piece for stream in streams for piece in stream.scratch()],
+        compiler_params=pltpu.CompilerParams(
+            collective_id=0, has_side_effects=True, vmem_limit_bytes=52 * 2**20
+        ),
+        cost_estimate=pl.CostEstimate(
+            flops=2 * size, bytes_accessed=8 * size, transcendentals=0
+        ),
+    )(*arrays)
+
+
+def sum_gradients(w_qkv_grad, w_out_grad, w_fc_grad, w_proj_grad, vectors):
+    if lax.axis_size("dp") != 16:
+        return lax.psum((w_qkv_grad, w_out_grad, w_fc_grad, w_proj_grad, vectors), "dp")
+    flat = jnp.concatenate([item.reshape(-1, 128) for item in vectors])
+    rows = flat.shape[0]
+    flat = jnp.pad(flat, ((0, -rows % 64), (0, 0)))
+    stacked = w_qkv_grad.reshape(-1, w_qkv_grad.shape[2])
+    proj, fc, qkv, out, flat = sum_over_data([w_proj_grad, w_fc_grad, stacked, w_out_grad, flat])
+    summed, start = [], 0
+    for item in vectors:
+        height = item.size // 128
+        summed.append(flat[start : start + height].reshape(item.shape))
+        start += height
+    return qkv.reshape(w_qkv_grad.shape), out, fc, proj, summed
 
 
 def per_device(
@@ -60,7 +406,6 @@
     rows = block_input.shape[0]
     local_width = w_qkv.shape[2]
     heads = local_width // HEAD_DIM
-    groups = lax.axis_size("dp")
     ends = jnp.cumsum(seq_lengths[0])
     position = jnp.arange(rows, dtype=jnp.int32)
     segment = jnp.sum((position[:, None] >= ends[None, :]).astype(jnp.int32), axis=1)
@@ -112,7 +457,6 @@
     grad_hidden = jax.vjp(gelu, hidden_pre)[1](grad_act)[0].astype(jnp.bfloat16)
     fc_bias_grad = jnp.sum(grad_hidden.astype(jnp.float32), axis=0)
     w_fc_grad = jnp.einsum("td,tf->df", normed_two, grad_hidden, preferred_element_type=jnp.float32)
-    mlp_list = [w_fc_grad, fc_bias_grad, w_proj_grad, proj_bias_grad]
     grad_normed_two = lax.psum(
         jnp.einsum("tf,df->td", grad_hidden, w_fc, preferred_element_type=jnp.float32), "tensor"
     )
@@ -166,35 +510,34 @@
         grad_normed_one
     )
     input_grad = (grad_residual + grad_in_ln).astype(jnp.bfloat16)
-    attn_list = [
+    vectors = [
         ln1_gain_grad,
         ln1_bias_grad,
-        w_qkv_grad,
         qv_bias_grad,
-        w_out_grad,
         out_bias_grad,
         ln2_gain_grad,
         ln2_bias_grad,
+        fc_bias_grad,
+        proj_bias_grad,
     ]
-    total_flat, total_padded = flatten_all(attn_list + mlp_list, groups)
-    share = lax.psum_scatter(total_flat, "dp", scatter_dimension=0, tiled=True)
-    gathered = lax.all_gather(share, "dp", axis=0, tiled=True)
-    summed = restore_all(gathered, attn_list + mlp_list)
+    w_qkv_grad, w_out_grad, w_fc_grad, w_proj_grad, vectors = sum_gradients(
+        w_qkv_grad, w_out_grad, w_fc_grad, w_proj_grad, vectors
+    )
     return (
         block_output,
         input_grad,
-        summed[0],
-        summed[1],
-        summed[2],
-        summed[3],
-        summed[4],
-        summed[5],
-        summed[6],
-        summed[7],
-        summed[8],
-        summed[9],
-        summed[10],
-        summed[11],
+        vectors[0],
+        vectors[1],
+        w_qkv_grad,
+        vectors[2],
+        w_out_grad,
+        vectors[3],
+        vectors[4],
+        vectors[5],
+        w_fc_grad,
+        vectors[6],
+        w_proj_grad,
+        vectors[7],
     )
 
 

time: 1570 us -> 1070 us (0.68)
  waiting for transfers between devices: 1350 us -> 37.8 us
  Pallas kernels: 0 us -> 906 us
  local copies, waits for them, and re-layouts: 147 us -> 47.5 us
    unnamed x7 -> x3, waiting for transfers between devices: 1310 us -> 0.05 us
    pallas_call x0 -> x1, Pallas kernels: none -> 906 us  [sum_over_data(): pl.pallas_call(functools.partial(reduce_kernel, streams), out_shape=[jax....]
    unnamed x118 -> x105, local copies, waits for them, and re-layouts: 75.2 us -> 25.6 us
    slice x8 -> x0, local copies, waits for them, and re-layouts: 34.9 us -> none  [restore_all(): result.append(flat[offset:offset + item.size].reshape(item.shape))]
  transfers between devices with their start and end apart: 5 -> 3, of which waited for: 4 -> 2; matrix products, arithmetic and copies ran while one was open for 3% -> 3% of each run, Pallas kernels for 0% -> 0%
where the time goes in v1:
time: 1070 us
  Pallas kernels  906 us (85%)
  local copies, waits for them, and re-layouts  47.5 us (4%)
  matrix products  47 us (4%)
  waiting for transfers between devices  37.8 us (4%)
  between operations  14.3 us (1%)
  other arithmetic  14 us (1%)
    pallas_call x1, Pallas kernels, sum_over_data(): pl.pallas_call(functools.partial(reduce_kernel, streams), out_shape=[jax....  906 us
    unnamed x105, local copies, waits for them, and re-layouts  25.6 us
    psum x1, waiting for transfers between devices, per_device(): lax.psum(jnp.dot(attended, w_out, preferred_element_type=jnp.float32), 't...  22.4 us
  transfers between devices with their start and end apart: 3, of which 2 were waited for; matrix products, arithmetic and copies ran while one was open for 3% of the time, Pallas kernels for 0%

profile of v1, /device:TPU:0, one launch (start us, length us, event | category | flops | bytes accessed | tf_op | source)
XLA Modules:
  0.0 1067.2 jit_solution(12812665377320351076)
XLA Ops:
  7.2 1.3 convert_reduce_fusion.1
  8.6 1.3 fusion.19
  9.9 2.1 convolution_bitcast_fusion.1
  14.4 2.1 copy.57
  17.6 2.1 copy.58
  19.7 1.7 fusion.48
  23.5 1.4 fusion.49
  25.0 22.4 %all-reduce.6.cloned.1.call-done = f32[256,1024]{1,0:T(8,128)} async-done(((f32[256,1024]{1,0:T(8,128)}), f32[256,1024]{1,0:T(8,128)}) %all-reduce.6.cloned.1.call-update) | async-done | bytes 1048592 | tf_op jit(solution)/shard_map/psum | solution.py:442
  47.4 1.6 fusion.46
  50.0 3.7 convolution_add_fusion
  53.7 4.4 convert_reduce_fusion
  59.1 2.3 fusion.50
  61.7 5.3 fusion.42
  67.0 15.4 %all-reduce.8.cloned.1.call-done = f32[256,1024]{1,0:T(8,128)} async-done(((f32[256,1024]{1,0:T(8,128)}), f32[256,1024]{1,0:T(8,128)}) %all-reduce.8.cloned.1.call-update) | async-done | bytes 1048592 | tf_op jit(solution)/shard_map/psum | solution.py:460
  82.4 2.0 multiply_reduce_fusion.1
  89.4 2.9 convert_reduce_fusion.4
  97.3 1.8 copy.65
  99.1 1.8 copy.66
  100.9 3.0 convolution_bitcast_fusion.2
  105.5 4.8 fusion.41.refs_1_
  110.4 5.0 fusion.34.refs_0_
  115.6 3.9 convolution_bitcast_fusion
  119.5 7.0 copy.69
  126.5 1.8 fusion.51.refs_3_
  128.3 1.6 fusion.43
  129.9 2.6 fusion.18
  132.6 906.3 %shard_map.254 = (f32[2048,1024]{1,0:T(8,128)}, f32[1024,2048]{1,0:T(8,128)}, f32[3072,512]{1,0:T(8,128)}, f32[512,1024]{1,0:T(8,128)}, f32[128,128]{1,0:T(8,128)S(1)}) custom-call(f32[2048,1024]{1,0:T(8,128)} %fusion.34.refs_0_, f32[1024,2048]{1,0:T(8,128)} %fusion.41.refs_1_, f32[3072,512]{1,0:T(8,128)} %bitcast.78, f32[512,1024]{1,0:T(8,128)} %fusion.51.refs_3_, ...), custom_call_target="tpu_custom_call" | custom-call | flops 12615680 | bytes 50462720 | tf_op jit(solution)/shard_map/pallas_call | solution.py:358
  1042.1 6.9 copy.90
  1049.0 1.3 copy.91
  1050.7 4.3 copy.92
  1054.9 1.5 slice-done.1
  1056.5 3.9 copy.93
  (149 shorter events, 23.2 us)
Async XLA Ops:
  7.2 2.8 copy-start
  7.2 40.2 %all-reduce.6.cloned.1.call-start = ((), (), s32[]{:S(2)}) async-start(), calls=%async_computation | async-start | bytes 2097152 | tf_op jit(solution)/shard_map/psum | solution.py:442
  17.6 4.2 copy-start.23
  22.8 24.6 %copy-start.37 = (f32[1024]{0:T(1024)S(1)}, f32[1024]{0:T(1024)}, u32[]{:S(2)}) copy-start(f32[1024]{0:T(1024)} %param.23) | copy-start | bytes 12292
  24.9 25.0 %copy-start.34 = (f32[1024]{0:T(1024)S(1)}, f32[1024]{0:T(1024)}, u32[]{:S(2)}) copy-start(f32[1024]{0:T(1024)} %param.24) | copy-start | bytes 12292
  25.0 25.0 %copy-start.35 = (f32[1024]{0:T(1024)S(1)}, f32[1024]{0:T(1024)}, u32[]{:S(2)}) copy-start(f32[1024]{0:T(1024)} %param.25) | copy-start | bytes 12292
  25.0 25.0 %copy-start.43 = (f32[2048]{0:T(1024)S(1)}, f32[2048]{0:T(1024)}, u32[]{:S(2)}) copy-start(f32[2048]{0:T(1024)} %param.27) | copy-start | bytes 24580
  25.0 57.4 %all-reduce.8.cloned.1.call-start = ((), (), s32[]{:S(2)}) async-start(), calls=%async_computation.1 | async-start | bytes 2097152 | tf_op jit(solution)/shard_map/psum | solution.py:460
  49.9 3.7 copy-start.15
  50.0 3.7 copy-start.42
  53.7 4.5 copy-start.21
  53.7 5.4 copy-start.41
  61.4 66.9 %all-reduce.10.cloned.1.call-start = ((), (), s32[]{:S(2)}) async-start(), calls=%async_computation.2 | async-start | bytes 4194304 | tf_op jit(solution)/shard_map/psum | solution.py:449
  84.5 2.5 copy-start.20
  89.3 2.9 copy-start.3
  89.4 2.9 copy-start.27
  105.5 4.8 copy-start.17
  105.5 4.8 copy-start.22
  110.3 5.3 copy-start.7
  110.3 5.3 copy-start.30
  110.3 5.3 copy-start.31
  110.3 5.3 copy-start.36
  110.3 5.3 copy-start.38
  119.5 7.0 copy-start.13
  119.5 7.0 copy-start.33
  126.5 3.4 copy-start.40
  132.6 907.5 %copy-start.9 = (f32[256,1024]{1,0:T(8,128)S(1)}, f32[256,1024]{1,0:T(8,128)}, u32[]{:S(2)}) copy-start(f32[256,1024]{1,0:T(8,128)} %copy-done.8) | copy-start | bytes 3145732
  1042.1 6.9 copy-start.25
  1042.1 8.6 copy-start.11
  1049.0 5.9 slice-start
  1050.7 5.8 slice-start.1
  1056.5 4.2 copy-start.1
  (18 other events, 26.7 us)
Sparse Core Ops, SparseCore 0:
  25.1 22.2 all-reduce.5
  61.5 20.7 all-reduce.7
  104.1 22.4 all-reduce.9
